TPU v7x, 32 devices: a whole 2x2x4 slice. The times are simulated.
32 devices in a mesh: expert: 4 (over y, core), dp: 8 (over z, x).
Axes of the slice: x: 2, y: 2, z: 4, core: 2. Of those that a mesh axis runs over, the one named last changes fastest.
Arguments:
- tokens: bfloat16 [4096, 2048], P(('expert', 'dp')), may hold values from -6 to 6
- out_grad: bfloat16 [4096, 2048], P(('expert', 'dp')), may hold values from -6 to 6
- expert_ids: int32 [4096, 1], P(('expert', 'dp')), may hold values from 0 to 15; in each aligned block of 128 rows (0 to 127, 128 to 255, ...) at most 12 rows name the same one
- combine_ints: int32 [4096, 8], P(('expert', 'dp')), may hold values from 1 to 15
- w_gate: bfloat16 [16, 2048, 384], P('expert'), may hold values from -0.125 to 0.125
- w_up: bfloat16 [16, 2048, 384], P('expert'), may hold values from -0.125 to 0.125
- w_down: bfloat16 [16, 384, 2048], P('expert'), may hold values from -0.3125 to 0.3125
Outputs:
- combined: bfloat16 [4096, 2048], P(('expert', 'dp'))
- dinput: bfloat16 [4096, 2048], P(('expert', 'dp'))
- grad_down: float32 [16, 384, 2048], P('expert', None, 'dp')
Inputs may be any that keep to these rules, and one draw needn't show every extreme that they name: `expert_ids`: each row names one expert of the window. Among the 128 rows of one device no expert is named more than 12 times, and in every draw some expert is named exactly 12 times by the rows of some device.
All inputs are finite; a program needn't handle non-finite values.
Results may differ from a plain program's by a relative error of at most 0.0057.
Values may be sent and summed in bfloat16 or wider, within the bound.
A program may use at most 64 MiB of HBM per device.

v0:
```python
import jax
import jax.numpy as jnp
from jax import lax
from jax.sharding import PartitionSpec as P

CAP = 12


def body(tokens, out_grad, expert_ids, combine_ints, w_gate, w_up, w_down):
    tok_rows, model_width = tokens.shape
    route_count = expert_ids.shape[1]
    groups = lax.axis_size("expert")
    local_count = w_gate.shape[0]
    experts = groups * local_count
    flat_ids = expert_ids.reshape(-1)
    onehot = (flat_ids[:, None] == jnp.arange(experts, dtype=jnp.int32)[None, :]).astype(jnp.int32)
    slot_rank = jnp.sum((jnp.cumsum(onehot, axis=0) - onehot) * onehot, axis=1)
    slot_index = flat_ids * CAP + slot_rank
    owner_row = jnp.arange(tok_rows * route_count, dtype=jnp.int32) // route_count
    all_weights = combine_ints.astype(jnp.float32)
    weights = (all_weights[:, :route_count] / jnp.sum(all_weights, axis=1, keepdims=True)).reshape(
        -1
    )
    scaled = (weights[:, None] * out_grad[owner_row].astype(jnp.float32)).astype(jnp.bfloat16)
    empty_buf = jnp.zeros((experts * CAP, model_width), jnp.bfloat16)
    send_rows = empty_buf.at[slot_index].set(tokens[owner_row])
    send_grads = empty_buf.at[slot_index].set(scaled)
    recv_rows, recv_grads = (
        lax.all_to_all(send_rows, "expert", split_axis=0, concat_axis=0, tiled=True),
        lax.all_to_all(send_grads, "expert", split_axis=0, concat_axis=0, tiled=True),
    )
    rows_four = recv_rows.reshape(groups, local_count, CAP, model_width)
    grads_four = recv_grads.reshape(groups, local_count, CAP, model_width)
    gate_act = jnp.einsum("slcd,ldf->slcf", rows_four, w_gate, preferred_element_type=jnp.float32)
    up_act = jnp.einsum("slcd,ldf->slcf", rows_four, w_up, preferred_element_type=jnp.float32)
    gate_sig = jax.nn.sigmoid(gate_act)
    gate_silu = gate_act * gate_sig
    hidden = (gate_silu * up_act).astype(jnp.bfloat16)
    result = jnp.einsum(
        "slcf,lfd->slcd", hidden, w_down, preferred_element_type=jnp.float32
    ).astype(jnp.bfloat16)
    returned = lax.all_to_all(
        result.reshape(-1, model_width), "expert", split_axis=0, concat_axis=0, tiled=True
    )
    dhidden = jnp.einsum("slcd,lfd->slcf", grads_four, w_down, preferred_element_type=jnp.float32)
    grad_gate = (dhidden * up_act * gate_sig * (1.0 + gate_act * (1.0 - gate_sig))).astype(
        jnp.bfloat16
    )
    grad_up = (dhidden * gate_silu).astype(jnp.bfloat16)
    slot_grad = (
        jnp.einsum("slcf,ldf->slcd", grad_gate, w_gate, preferred_element_type=jnp.float32)
        + jnp.einsum("slcf,ldf->slcd", grad_up, w_up, preferred_element_type=jnp.float32)
    ).astype(jnp.bfloat16)
    grad_back = lax.all_to_all(
        slot_grad.reshape(-1, model_width), "expert", split_axis=0, concat_axis=0, tiled=True
    )
    grad_term = jnp.einsum("slcf,slcd->lfd", hidden, grads_four, preferred_element_type=jnp.float32)
    grad_share = lax.psum_scatter(grad_term, "dp", scatter_dimension=2, tiled=True)
    combined = jnp.sum(
        (weights[:, None] * returned[slot_index].astype(jnp.float32)).reshape(
            tok_rows, route_count, model_width
        ),
        axis=1,
    ).astype(jnp.bfloat16)
    dinput = jnp.sum(
        grad_back[slot_index].astype(jnp.float32).reshape(tok_rows, route_count, model_width),
        axis=1,
    ).astype(jnp.bfloat16)
    return (combined, dinput, grad_share)


def solution(mesh):
    return jax.shard_map(
        body,
        mesh=mesh,
        in_specs=(
            P(("expert", "dp"), None),
            P(("expert", "dp"), None),
            P(("expert", "dp"), None),
            P(("expert", "dp"), None),
            P("expert", None, None),
            P("expert", None, None),
            P("expert", None, None),
        ),
        out_specs=(P(("expert", "dp"), None), P(("expert", "dp"), None), P("expert", None, "dp")),
        check_vma=False,
    )
```

profile of v0, /device:TPU:0, one launch (start us, length us, event | category | flops | bytes accessed | tf_op | source)
XLA Modules:
  0.0 270.3 jit_solution(3683196120391407520)
XLA Ops:
  7.2 0.0 copy-start
  7.2 0.8 fusion.49
  8.0 0.2 reduce_window_sum.11
  8.2 0.8 select_reduce_fusion
  9.0 0.7 fusion.50
  9.7 0.0 copy-done
  9.7 3.9 %scatter_custom_fusion = bf16[192,2048]{1,0:T(8,128)(2,1)} fusion(s32[128]{0:T(128)S(1)} %fusion.50, bf16[128,2048]{1,0:T(8,128)(2,1)S(1)} %copy-done, s32[1024]{0:T(1024)S(1)} %pad_clamp_fusion.1, bf16[]{:T(256)} %constant.25.clone.1), kind=kCustom, calls=%fused_computation.34 | custom fusion | bytes 786434 | tf_op jit(solution)/shard_map/scatter | solution.py:26
  13.6 4.2 %all-to-all-start = ((bf16[4,48,2048]{2,1,0:T(8,128)(2,1)}), bf16[4,48,2048]{2,1,0:T(8,128)(2,1)S(1)}, u32[]{:S(2)}, u32[]{:S(2)}) async-start(bf16[4,48,2048]{2,1,0:T(8,128)(2,1)} %bitcast.5), calls=%async_computation | async-start | bytes 1572864 | tf_op jit(solution)/shard_map/all_to_all | solution.py:29
  17.8 0.0 slice-start
  17.9 0.8 convert_element_type.45
  18.7 0.7 convert_reduce_fusion
  19.4 4.5 %scatter_custom_fusion.1 = bf16[192,2048]{1,0:T(8,128)(2,1)} fusion(s32[128]{0:T(128)S(1)} %fusion.50, f32[128]{0:T(128)S(1)} %fusion.51, bf16[]{:T(256)} %constant.25.clone.1, bf16[128,2048]{1,0:T(8,128)(2,1)} %param.8, s32[1024]{0:T(1024)S(1)} %pad_clamp_fusion.1), kind=kCustom, calls=%fused_computation.33 | custom fusion | flops 786432 | bytes 1315330 | tf_op jit(solution)/shard_map/scatter | solution.py:27
  23.9 5.6 %all-to-all-done = bf16[4,48,2048]{2,1,0:T(8,128)(2,1)S(1)} async-done(((bf16[4,48,2048]{2,1,0:T(8,128)(2,1)}), bf16[4,48,2048]{2,1,0:T(8,128)(2,1)S(1)}, u32[]{:S(2)}, u32[]{:S(2)}) %all-to-all-start) | async-done | bytes 786464 | tf_op jit(solution)/shard_map/all_to_all | solution.py:29
  29.5 4.2 %all-to-all-start.2 = ((bf16[4,48,2048]{2,1,0:T(8,128)(2,1)}), bf16[4,48,2048]{2,1,0:T(8,128)(2,1)}, u32[]{:S(2)}, u32[]{:S(2)}) async-start(bf16[4,48,2048]{2,1,0:T(8,128)(2,1)} %bitcast.87), calls=%async_computation.2 | async-start | bytes 1572864 | tf_op jit(solution)/shard_map/all_to_all | solution.py:30
  33.7 0.2 reduce-scatter.2.cloned.1.call-start
  33.9 0.6 copy.28
  34.5 0.0 slice-start.1
  34.6 4.3 %fusion.30 = f32[4,4,12,384]{3,2,0,1:T(8,128)S(1)} fusion(bf16[4,2048,384]{2,1,0:T(8,128)(2,1)} %param.11, bf16[4,4,12,2048]{3,0,2,1:T(4,128)(2,1)S(1)} %bitcast.81), kind=kOutput, calls=%fused_computation.25 | convolution fusion | flops 301989888 | bytes 7372800 | tf_op jit(solution)/shard_map/slcd,ldf->slcf/dot_general | solution.py:34
  38.8 0.0 slice-done
  38.8 0.0 slice-done.1
  38.9 2.1 multiply_convert_fusion.5
  40.9 4.5 %all-to-all-done.2 = bf16[4,48,2048]{2,1,0:T(8,128)(2,1)} async-done(((bf16[4,48,2048]{2,1,0:T(8,128)(2,1)}), bf16[4,48,2048]{2,1,0:T(8,128)(2,1)}, u32[]{:S(2)}, u32[]{:S(2)}) %all-to-all-start.2) | async-done | bytes 786464 | tf_op jit(solution)/shard_map/all_to_all | solution.py:30
  45.4 1.7 copy.33
  47.2 7.3 %convolution_bitcast_fusion = f32[4,384,2048]{2,1,0:T(8,128)} fusion(bf16[4,4,12,384]{3,2,0,1:T(8,128)(2,1)} %get-tuple-element.3, bf16[4,4,12,2048]{3,0,2,1:T(4,128)(2,1)S(1)} %bitcast.83), kind=kOutput, calls=%fused_computation.18 | convolution fusion | flops 301989888 | bytes 13516800 | tf_op jit(solution)/shard_map/slcf,slcd->lfd/dot_general | solution.py:57
  54.5 0.0 reduce-scatter.2.cloned.1.call-update
  54.5 0.0 slice-start.2
  54.5 5.0 %fusion.27 = f32[4,4,12,384]{3,2,0,1:T(8,128)S(1)} fusion(bf16[4,384,2048]{2,1,0:T(8,128)(2,1)} %param.13, bf16[4,4,12,2048]{3,0,2,1:T(4,128)(2,1)S(1)} %bitcast.84), kind=kOutput, calls=%fused_computation.24 | convolution fusion | flops 301989888 | bytes 7372800 | tf_op jit(solution)/shard_map/slcd,lfd->slcf/dot_general | solution.py:45
  59.5 0.0 slice-start.3
  59.6 5.0 %fusion = f32[4,4,12,2048]{3,2,1,0:T(8,128)S(1)} fusion(bf16[4,2048,384]{2,1,0:T(8,128)(2,1)} %param.12, f32[4,4,12,384]{3,2,0,1:T(8,128)S(1)} %fusion.27, f32[4,4,12,384]{3,2,0,1:T(8,128)S(1)} %fusion.30), kind=kOutput, calls=%fused_computation.6 | convolution fusion | flops 302432256 | bytes 8454144 | tf_op jit(solution)/shard_map/slcf,ldf->slcd/dot_general | solution.py:52
  64.6 0.0 slice-done.2
  64.6 0.0 slice-done.3
  64.6 0.0 copy-start.1
  64.6 2.1 fusion.24
  66.8 0.6 copy.35
  67.4 1.3 copy.36
  68.7 3.7 %all-to-all-start.3 = ((bf16[4,48,2048]{2,1,0:T(8,128)(2,1)}), bf16[4,48,2048]{2,1,0:T(8,128)(2,1)S(1)}, u32[]{:S(2)}, u32[]{:S(2)}) async-start(bf16[4,48,2048]{2,1,0:T(8,128)(2,1)} %copy.36), calls=%async_computation.3 | async-start | bytes 1572864 | tf_op jit(solution)/shard_map/all_to_all | solution.py:54
  72.4 0.0 copy-done.1
  72.4 4.0 %fusion.21 = bf16[4,4,12,2048]{3,2,0,1:T(8,128)(2,1)S(1)} fusion(bf16[4,4,12,384]{3,2,0,1:T(8,128)(2,1)S(1)} %copy-done.1, bf16[4,384,2048]{2,1,0:T(8,128)(2,1)} %param.13), kind=kOutput, calls=%fused_computation.22 | convolution fusion | flops 302383104 | bytes 7225344 | tf_op jit(solution)/shard_map/slcf,lfd->slcd/dot_general | solution.py:39
  76.5 0.6 copy.31
  77.1 1.4 copy.32
  78.5 5.4 %all-to-all-done.3 = bf16[4,48,2048]{2,1,0:T(8,128)(2,1)S(1)} async-done(((bf16[4,48,2048]{2,1,0:T(8,128)(2,1)}), bf16[4,48,2048]{2,1,0:T(8,128)(2,1)S(1)}, u32[]{:S(2)}, u32[]{:S(2)}) %all-to-all-start.3) | async-done | bytes 786464 | tf_op jit(solution)/shard_map/all_to_all | solution.py:54
  83.8 3.5 %all-to-all-start.1 = ((bf16[4,48,2048]{2,1,0:T(8,128)(2,1)}), bf16[4,48,2048]{2,1,0:T(8,128)(2,1)S(1)}, u32[]{:S(2)}, u32[]{:S(2)}) async-start(bf16[4,48,2048]{2,1,0:T(8,128)(2,1)} %copy.32), calls=%async_computation.1 | async-start | bytes 1572864 | tf_op jit(solution)/shard_map/all_to_all | solution.py:42
  87.3 1.7 gather_fusion.1
  89.1 9.9 %all-to-all-done.1 = bf16[4,48,2048]{2,1,0:T(8,128)(2,1)S(1)} async-done(((bf16[4,48,2048]{2,1,0:T(8,128)(2,1)}), bf16[4,48,2048]{2,1,0:T(8,128)(2,1)S(1)}, u32[]{:S(2)}, u32[]{:S(2)}) %all-to-all-start.1) | async-done | bytes 786464 | tf_op jit(solution)/shard_map/all_to_all | solution.py:42
  99.0 0.9 gather_fusion
  99.9 0.9 multiply_convert_fusion.1
  100.8 162.6 %reduce-scatter.2.cloned.1.call-done = f32[4,384,256]{2,1,0:T(8,128)} async-done(((f32[4,384,2048]{2,1,0:T(8,128)}), f32[4,384,256]{2,1,0:T(8,128)}) %reduce-scatter.2.cloned.1.call-update) | async-done | bytes 1572880 | tf_op jit(solution)/shard_map/reduce_scatter | solution.py:58
  (6 shorter events, 0.0 us)
Async XLA Ops:
  7.2 2.5 copy-start
  13.6 15.9 %all-to-all-start = ((bf16[4,48,2048]{2,1,0:T(8,128)(2,1)}), bf16[4,48,2048]{2,1,0:T(8,128)(2,1)S(1)}, u32[]{:S(2)}, u32[]{:S(2)}) async-start(bf16[4,48,2048]{2,1,0:T(8,128)(2,1)} %bitcast.5), calls=%async_computation | async-start | bytes 1572864 | tf_op jit(solution)/shard_map/all_to_all | solution.py:29
  17.8 21.0 %slice-start = ((s8[6291456]{0:T(1024)(128)(4,1)}), s8[2097152]{0:T(1024)(128)(4,1)S(1)}, s32[]{:S(2)}) async-start(s8[6291456]{0:T(1024)(128)(4,1)} %bitcast.77), calls=%async_computation.6 | async-start | bytes 4194304
  29.5 15.9 %all-to-all-start.2 = ((bf16[4,48,2048]{2,1,0:T(8,128)(2,1)}), bf16[4,48,2048]{2,1,0:T(8,128)(2,1)}, u32[]{:S(2)}, u32[]{:S(2)}) async-start(bf16[4,48,2048]{2,1,0:T(8,128)(2,1)} %bitcast.87), calls=%async_computation.2 | async-start | bytes 1572864 | tf_op jit(solution)/shard_map/all_to_all | solution.py:30
  33.7 229.7 %reduce-scatter.2.cloned.1.call-start = ((), (), s32[]{:S(2)}) async-start(), calls=%async_computation.5 | async-start | bytes 14155776 | tf_op jit(solution)/shard_map/reduce_scatter | solution.py:58
  34.5 4.3 %slice-start.1 = ((s8[6291456]{0:T(1024)(128)(4,1)}), s8[4194304]{0:T(1024)(128)(4,1)S(1)}, s32[]{:S(2)}) async-start(s8[6291456]{0:T(1024)(128)(4,1)} %bitcast.77), calls=%async_computation.7 | async-start | bytes 8388608
  54.5 10.1 %slice-start.2 = ((s8[6291456]{0:T(1024)(128)(4,1)}), s8[4194304]{0:T(1024)(128)(4,1)S(1)}, s32[]{:S(2)}) async-start(s8[6291456]{0:T(1024)(128)(4,1)} %bitcast.79), calls=%async_computation.8 | async-start | bytes 8388608
  59.5 5.1 %slice-start.3 = ((s8[6291456]{0:T(1024)(128)(4,1)}), s8[2097152]{0:T(1024)(128)(4,1)S(1)}, s32[]{:S(2)}) async-start(s8[6291456]{0:T(1024)(128)(4,1)} %bitcast.79), calls=%async_computation.9 | async-start | bytes 4194304
  64.6 7.8 %copy-start.1 = (bf16[4,4,12,384]{3,2,0,1:T(8,128)(2,1)S(1)}, bf16[4,4,12,384]{3,2,0,1:T(8,128)(2,1)}, u32[]{:S(2)}) copy-start(bf16[4,4,12,384]{3,2,0,1:T(8,128)(2,1)} %get-tuple-element.3) | copy-start | bytes 442372
  68.7 15.1 %all-to-all-start.3 = ((bf16[4,48,2048]{2,1,0:T(8,128)(2,1)}), bf16[4,48,2048]{2,1,0:T(8,128)(2,1)S(1)}, u32[]{:S(2)}, u32[]{:S(2)}) async-start(bf16[4,48,2048]{2,1,0:T(8,128)(2,1)} %copy.36), calls=%async_computation.3 | async-start | bytes 1572864 | tf_op jit(solution)/shard_map/all_to_all | solution.py:54
  83.8 15.1 %all-to-all-start.1 = ((bf16[4,48,2048]{2,1,0:T(8,128)(2,1)}), bf16[4,48,2048]{2,1,0:T(8,128)(2,1)S(1)}, u32[]{:S(2)}, u32[]{:S(2)}) async-start(bf16[4,48,2048]{2,1,0:T(8,128)(2,1)} %copy.32), calls=%async_computation.1 | async-start | bytes 1572864 | tf_op jit(solution)/shard_map/all_to_all | solution.py:42
Sparse Core Ops, SparseCore 0:
  54.6 208.7 reduce-scatter.1
where the time goes:
time: 271 us; the launch traced here: 270 us
  waiting for transfers between devices  188 us (69%)
  matrix products  29.8 us (11%)
  starting transfers between devices  15.8 us (6%)
  between operations  14.2 us (5%)
  local copies, waits for them, and re-layouts  12.9 us (5%)
  other arithmetic  9.45 us (3%)
    reduce_scatter x1, waiting for transfers between devices, body(): lax.psum_scatter(grad_term, 'dp', scatter_dimension=2, tiled=True)  163 us
    all_to_all x1, waiting for transfers between devices, body(): lax.all_to_all(result.reshape(-1, model_width), 'expert', split_axis=0, c...  9.88 us
    dot_general x1, matrix products, body(): jnp.einsum('slcf,slcd->lfd', hidden, grads_four, preferred_element_type=j...  7.35 us
    all_to_all x1, waiting for transfers between devices, body(): lax.all_to_all(send_rows, 'expert', split_axis=0, concat_axis=0, tiled=True)  5.63 us
  transfers between devices with their start and end apart: 5, of which 5 were waited for; matrix products, arithmetic and copies ran while one was open for 14% of the time, Pallas kernels for 0%

commit v1 on v0

--- a/solution.py
+++ b/solution.py
@@ -54,8 +54,15 @@
     grad_back = lax.all_to_all(
         slot_grad.reshape(-1, model_width), "expert", split_axis=0, concat_axis=0, tiled=True
     )
-    grad_term = jnp.einsum("slcf,slcd->lfd", hidden, grads_four, preferred_element_type=jnp.float32)
-    grad_share = lax.psum_scatter(grad_term, "dp", scatter_dimension=2, tiled=True)
+    parts = lax.axis_size("dp")
+    cols = model_width // parts
+    hidden_all = lax.all_gather(hidden, "dp", axis=0, tiled=False)
+    grad_cols = lax.all_to_all(
+        grads_four.reshape(-1, parts, cols).transpose(1, 0, 2), "dp", split_axis=0, concat_axis=0, tiled=True
+    ).reshape(parts, groups, local_count, CAP, cols)
+    grad_share = jnp.einsum(
+        "pslcf,pslcd->lfd", hidden_all, grad_cols, preferred_element_type=jnp.float32
+    )
     combined = jnp.sum(
         (weights[:, None] * returned[slot_index].astype(jnp.float32)).reshape(
             tok_rows, route_count, model_width

time: 271 us -> 141 us (0.52)
  waiting for transfers between devices: 188 us -> 56.4 us
  starting transfers between devices: 15.8 us -> 21.4 us
  matrix products: 29.8 us -> 25.8 us
    reduce_scatter x1 -> x0, waiting for transfers between devices: 163 us -> none  [body(): lax.psum_scatter(grad_term, 'dp', scatter_dimension=2, tiled=True)]
    all_to_all x0 -> x1, waiting for transfers between devices: none -> 27.2 us  [body(): lax.all_to_all(grads_four.reshape(-1, parts, cols).transpose(1, 0, 2), 'd...]
    all_to_all x0 -> x1, starting transfers between devices: none -> 6.47 us  [body(): lax.all_to_all(grads_four.reshape(-1, parts, cols).transpose(1, 0, 2), 'd...]
    dot_general x1, matrix products: 7.35 us -> 3.42 us  [body(): jnp.einsum('pslcf,pslcd->lfd', hidden_all, grad_cols, preferred_element_t...]
    dot_general x1, matrix products: 2.06 us -> 5.01 us  [body(): jnp.einsum('slcd,ldf->slcf', rows_four, w_up, preferred_element_type=jnp....]
    dot_general x1, matrix products: 5.02 us -> 2.1 us  [body(): jnp.einsum('slcf,ldf->slcd', grad_up, w_up, preferred_element_type=jnp.fl...]
    all_to_all x1, waiting for transfers between devices: 4.5 us -> 7.26 us  [body(): lax.all_to_all(send_grads, 'expert', split_axis=0, concat_axis=0, tiled=T...]
  transfers between devices with their start and end apart: 5 -> 6, of which waited for: 5 -> 5; matrix products, arithmetic and copies ran while one was open for 14% -> 15% of each run, Pallas kernels for 0% -> 0%
where the time goes in v1:
time: 141 us; the launch traced here: 140 us
  waiting for transfers between devices  56.4 us (40%)
  matrix products  25.8 us (18%)
  starting transfers between devices  21.4 us (15%)
  between operations  14.2 us (10%)
  local copies, waits for them, and re-layouts  13.8 us (10%)
  other arithmetic  8.83 us (6%)
    all_to_all x1, waiting for transfers between devices, body(): lax.all_to_all(grads_four.reshape(-1, parts, cols).transpose(1, 0, 2), 'd...  27.2 us
    all_to_all x1, waiting for transfers between devices, body(): lax.all_to_all(result.reshape(-1, model_width), 'expert', split_axis=0, c...  10.4 us
    all_to_all x1, waiting for transfers between devices, body(): lax.all_to_all(send_grads, 'expert', split_axis=0, concat_axis=0, tiled=T...  7.26 us
    all_to_all x1, starting transfers between devices, body(): lax.all_to_all(grads_four.reshape(-1, parts, cols).transpose(1, 0, 2), 'd...  6.47 us
    all_to_all x1, waiting for transfers between devices, body(): lax.all_to_all(send_rows, 'expert', split_axis=0, concat_axis=0, tiled=True)  5.94 us
    dot_general x1, matrix products, body(): jnp.einsum('slcd,ldf->slcf', rows_four, w_up, preferred_element_type=jnp....  5.01 us
    all_to_all x1, waiting for transfers between devices, body(): lax.all_to_all(slot_grad.reshape(-1, model_width), 'expert', split_axis=0...  4.91 us
    dot_general x1, matrix products, body(): jnp.einsum('slcd,lfd->slcf', grads_four, w_down, preferred_element_type=j...  4.88 us
  transfers between devices with their start and end apart: 6, of which 5 were waited for; matrix products, arithmetic and copies ran while one was open for 15% of the time, Pallas kernels for 0%

profile of v1, /device:TPU:0, one launch (start us, length us, event | category | flops | bytes accessed | tf_op | source)
XLA Modules:
  0.0 140.5 jit_solution(15626616978924072623)
XLA Ops:
  7.2 0.0 copy-start
  7.2 0.7 convert_element_type.45
  7.9 0.7 convert_reduce_fusion
  8.6 0.7 fusion.54
  9.4 0.2 reduce_window_sum.11
  9.5 0.8 select_reduce_fusion
  10.4 0.7 fusion.55
  11.1 0.0 copy-done
  11.1 4.0 %scatter_custom_fusion.1 = bf16[192,2048]{1,0:T(8,128)(2,1)} fusion(s32[128]{0:T(128)S(1)} %fusion.55, f32[128]{0:T(128)S(1)} %fusion.56, bf16[]{:T(256)} %constant.25.clone.1, bf16[128,2048]{1,0:T(8,128)(2,1)S(1)} %copy-done, s32[1024]{0:T(1024)S(1)} %pad_clamp_fusion.1), kind=kCustom, calls=%fused_computation.36 | custom fusion | flops 786432 | bytes 1315330 | tf_op jit(solution)/shard_map/scatter | solution.py:27
  15.1 4.2 %all-to-all-start.2 = ((bf16[4,48,2048]{2,1,0:T(8,128)(2,1)}), bf16[4,48,2048]{2,1,0:T(8,128)(2,1)S(1)}, u32[]{:S(2)}, u32[]{:S(2)}) async-start(bf16[4,48,2048]{2,1,0:T(8,128)(2,1)} %bitcast.18), calls=%async_computation.2 | async-start | bytes 1572864 | tf_op jit(solution)/shard_map/all_to_all | solution.py:30
  19.3 4.4 %scatter_custom_fusion = bf16[192,2048]{1,0:T(8,128)(2,1)} fusion(s32[128]{0:T(128)S(1)} %fusion.55, bf16[128,2048]{1,0:T(8,128)(2,1)} %param.7, s32[1024]{0:T(1024)S(1)} %pad_clamp_fusion.1, bf16[]{:T(256)} %constant.25.clone.1), kind=kCustom, calls=%fused_computation.37 | custom fusion | bytes 786944 | tf_op jit(solution)/shard_map/scatter | solution.py:26
  23.7 7.3 %all-to-all-done.2 = bf16[4,48,2048]{2,1,0:T(8,128)(2,1)S(1)} async-done(((bf16[4,48,2048]{2,1,0:T(8,128)(2,1)}), bf16[4,48,2048]{2,1,0:T(8,128)(2,1)S(1)}, u32[]{:S(2)}, u32[]{:S(2)}) %all-to-all-start.2) | async-done | bytes 786464 | tf_op jit(solution)/shard_map/all_to_all | solution.py:30
  31.0 3.7 %all-to-all-start = ((bf16[4,48,2048]{2,1,0:T(8,128)(2,1)}), bf16[4,48,2048]{2,1,0:T(8,128)(2,1)S(1)}, u32[]{:S(2)}, u32[]{:S(2)}) async-start(bf16[4,48,2048]{2,1,0:T(8,128)(2,1)} %bitcast.5), calls=%async_computation | async-start | bytes 1572864 | tf_op jit(solution)/shard_map/all_to_all | solution.py:29
  34.7 0.6 copy.35
  35.3 4.9 %fusion.32 = f32[4,4,12,384]{3,2,0,1:T(8,128)S(1)} fusion(bf16[4,384,2048]{2,1,0:T(8,128)(2,1)} %param.13, bf16[4,4,12,2048]{3,0,2,1:T(4,128)(2,1)S(1)} %bitcast.92), kind=kOutput, calls=%fused_computation.26 | convolution fusion | flops 301989888 | bytes 7372800 | tf_op jit(solution)/shard_map/slcd,lfd->slcf/dot_general | solution.py:45
  40.2 5.9 %all-to-all-done = bf16[4,48,2048]{2,1,0:T(8,128)(2,1)S(1)} async-done(((bf16[4,48,2048]{2,1,0:T(8,128)(2,1)}), bf16[4,48,2048]{2,1,0:T(8,128)(2,1)S(1)}, u32[]{:S(2)}, u32[]{:S(2)}) %all-to-all-start) | async-done | bytes 786464 | tf_op jit(solution)/shard_map/all_to_all | solution.py:29
  46.1 0.6 copy.30
  46.7 0.0 slice-start
  46.7 4.3 %fusion.35 = f32[4,4,12,384]{3,2,0,1:T(8,128)S(1)} fusion(bf16[4,2048,384]{2,1,0:T(8,128)(2,1)} %param.11, bf16[4,4,12,2048]{3,0,2,1:T(4,128)(2,1)S(1)} %bitcast.89), kind=kOutput, calls=%fused_computation.27 | convolution fusion | flops 301989888 | bytes 7372800 | tf_op jit(solution)/shard_map/slcd,ldf->slcf/dot_general | solution.py:34
  51.0 0.0 slice-start.1
  51.0 0.0 slice-start.2
  51.0 5.0 %multiply_convert_fusion.5 = (bf16[4,4,12,384]{3,2,0,1:T(8,128)(2,1)}, f32[4,4,12,384]{3,2,0,1:T(8,128)S(1)}) fusion(f32[4,4,12,384]{3,2,0,1:T(8,128)S(1)} %fusion.35, bf16[4,2048,384]{2,1,0:T(8,128)(2,1)} %param.12, bf16[4,4,12,2048]{3,0,2,1:T(4,128)(2,1)S(1)} %bitcast.90), kind=kOutput, calls=%fused_computation.42 | convolution fusion | flops 302432256 | bytes 7815168 | tf_op jit(solution)/shard_map/slcd,ldf->slcf/dot_general | solution.py:35
  56.0 0.0 slice-done
  56.0 0.0 slice-done.1
  56.0 0.0 slice-start.3
  56.0 2.1 %fusion = f32[4,4,12,2048]{3,2,1,0:T(8,128)S(1)} fusion(bf16[4,2048,384]{2,1,0:T(8,128)(2,1)S(1)} %bitcast.86, f32[4,4,12,384]{3,2,0,1:T(8,128)S(1)} %fusion.32, f32[4,4,12,384]{3,2,0,1:T(8,128)S(1)} %fusion.35), kind=kOutput, calls=%fused_computation.6 | convolution fusion | flops 302432256 | bytes 8454144 | tf_op jit(solution)/shard_map/slcf,ldf->slcd/dot_general | solution.py:52
  58.2 0.0 slice-done.2
  58.2 0.0 slice-done.3
  58.2 0.0 copy-start.1
  58.2 2.1 %fusion.24 = bf16[4,4,12,2048]{3,2,0,1:T(8,128)(2,1)S(1)} fusion(f32[4,4,12,2048]{3,2,1,0:T(8,128)S(1)} %fusion, bf16[4,2048,384]{2,1,0:T(8,128)(2,1)S(1)} %bitcast.88, f32[4,4,12,384]{3,2,0,1:T(8,128)S(1)} %fusion.35, f32[4,4,12,384]{3,2,0,1:T(8,128)S(1)} %fusion.32, f32[4,4,12,384]{3,2,0,1:T(8,128)S(1)} %get-tuple-element.4), kind=kOutput, calls=%fused_computation.22 | convolution fusion | flops 303513600 | bytes 9535488 | tf_op jit(solution)/shard_map/slcf,ldf->slcd/dot_general | solution.py:51
  60.3 0.6 copy.37
  60.9 1.3 copy.38
  62.2 3.5 %all-to-all-start.3 = ((bf16[4,48,2048]{2,1,0:T(8,128)(2,1)}), bf16[4,48,2048]{2,1,0:T(8,128)(2,1)S(1)}, u32[]{:S(2)}, u32[]{:S(2)}) async-start(bf16[4,48,2048]{2,1,0:T(8,128)(2,1)} %copy.38), calls=%async_computation.3 | async-start | bytes 1572864 | tf_op jit(solution)/shard_map/all_to_all | solution.py:54
  65.7 0.0 all-gather.3.cloned.1.call-start
  65.8 0.7 all-gather.3.cloned.1.call-update
  66.5 0.0 copy-done.1
  66.5 4.0 %fusion.21 = bf16[4,4,12,2048]{3,2,0,1:T(8,128)(2,1)S(1)} fusion(bf16[4,4,12,384]{3,2,0,1:T(8,128)(2,1)S(1)} %copy-done.1, bf16[4,384,2048]{2,1,0:T(8,128)(2,1)} %param.13), kind=kOutput, calls=%fused_computation.21 | convolution fusion | flops 302383104 | bytes 7225344 | tf_op jit(solution)/shard_map/slcf,lfd->slcd/dot_general | solution.py:39
  70.5 0.6 copy.33
  71.1 1.3 copy.34
  72.4 4.9 %all-to-all-done.3 = bf16[4,48,2048]{2,1,0:T(8,128)(2,1)S(1)} async-done(((bf16[4,48,2048]{2,1,0:T(8,128)(2,1)}), bf16[4,48,2048]{2,1,0:T(8,128)(2,1)S(1)}, u32[]{:S(2)}, u32[]{:S(2)}) %all-to-all-start.3) | async-done | bytes 786464 | tf_op jit(solution)/shard_map/all_to_all | solution.py:54
  77.4 3.5 %all-to-all-start.1 = ((bf16[4,48,2048]{2,1,0:T(8,128)(2,1)}), bf16[4,48,2048]{2,1,0:T(8,128)(2,1)S(1)}, u32[]{:S(2)}, u32[]{:S(2)}) async-start(bf16[4,48,2048]{2,1,0:T(8,128)(2,1)} %copy.34), calls=%async_computation.1 | async-start | bytes 1572864 | tf_op jit(solution)/shard_map/all_to_all | solution.py:42
  80.9 0.2 copy.47
  81.1 1.0 copy.63
  82.1 10.4 %all-to-all-done.1 = bf16[4,48,2048]{2,1,0:T(8,128)(2,1)S(1)} async-done(((bf16[4,48,2048]{2,1,0:T(8,128)(2,1)}), bf16[4,48,2048]{2,1,0:T(8,128)(2,1)S(1)}, u32[]{:S(2)}, u32[]{:S(2)}) %all-to-all-start.1) | async-done | bytes 786464 | tf_op jit(solution)/shard_map/all_to_all | solution.py:42
  92.5 6.5 %all-to-all-start.4 = ((bf16[8,192,256]{2,1,0:T(8,128)(2,1)}), bf16[8,192,256]{2,1,0:T(8,128)(2,1)S(1)}, u32[]{:S(2)}, u32[]{:S(2)}) async-start(bf16[8,192,256]{2,1,0:T(8,128)(2,1)} %bitcast.82), calls=%async_computation.4 | async-start | bytes 1572864 | tf_op jit(solution)/shard_map/all_to_all | solution.py:60
  99.0 1.7 %gather_fusion.1 = bf16[128,2048]{1,0:T(8,128)(2,1)} fusion(bf16[192,2048]{1,0:T(8,128)(2,1)S(1)} %bitcast.83, s32[1024]{0:T(1024)S(1)} %pad_clamp_fusion), kind=kCustom, calls=%fused_computation.3 | custom fusion | bytes 1049088 | tf_op jit(solution)/shard_map/gather | solution.py:73
  100.7 0.9 gather_fusion
  101.6 0.9 multiply_convert_fusion.1
  102.6 27.2 %all-to-all-done.4 = bf16[8,192,256]{2,1,0:T(8,128)(2,1)S(1)} async-done(((bf16[8,192,256]{2,1,0:T(8,128)(2,1)}), bf16[8,192,256]{2,1,0:T(8,128)(2,1)S(1)}, u32[]{:S(2)}, u32[]{:S(2)}) %all-to-all-start.4) | async-done | bytes 786464 | tf_op jit(solution)/shard_map/all_to_all | solution.py:60
  129.8 0.4 copy.40
  130.2 0.0 all-gather.3.cloned.1.call-done
  130.2 3.4 %fusion.29 = f32[4,384,256]{2,1,0:T(8,128)} fusion(bf16[8,4,4,12,384]{4,3,1,0,2:T(8,128)(2,1)} %bitcast.99, bf16[8,4,4,12,256]{4,0,3,2,1:T(8,128)(2,1)S(1)} %bitcast.96), kind=kOutput, calls=%fused_computation.25 | convolution fusion | flops 301989888 | bytes 3538944 | tf_op jit(solution)/shard_map/pslcf,pslcd->lfd/dot_general | solution.py:63
  (6 shorter events, 0.0 us)
Async XLA Ops:
  7.2 3.9 %copy-start = (bf16[128,2048]{1,0:T(8,128)(2,1)S(1)}, bf16[128,2048]{1,0:T(8,128)(2,1)}, u32[]{:S(2)}) copy-start(bf16[128,2048]{1,0:T(8,128)(2,1)} %param.8) | copy-start | bytes 1572868
  15.1 15.9 %all-to-all-start.2 = ((bf16[4,48,2048]{2,1,0:T(8,128)(2,1)}), bf16[4,48,2048]{2,1,0:T(8,128)(2,1)S(1)}, u32[]{:S(2)}, u32[]{:S(2)}) async-start(bf16[4,48,2048]{2,1,0:T(8,128)(2,1)} %bitcast.18), calls=%async_computation.2 | async-start | bytes 1572864 | tf_op jit(solution)/shard_map/all_to_all | solution.py:30
  31.0 15.1 %all-to-all-start = ((bf16[4,48,2048]{2,1,0:T(8,128)(2,1)}), bf16[4,48,2048]{2,1,0:T(8,128)(2,1)S(1)}, u32[]{:S(2)}, u32[]{:S(2)}) async-start(bf16[4,48,2048]{2,1,0:T(8,128)(2,1)} %bitcast.5), calls=%async_computation | async-start | bytes 1572864 | tf_op jit(solution)/shard_map/all_to_all | solution.py:29
  46.7 9.3 %slice-start = ((s8[6291456]{0:T(1024)(128)(4,1)}), s8[4194304]{0:T(1024)(128)(4,1)S(1)}, s32[]{:S(2)}) async-start(s8[6291456]{0:T(1024)(128)(4,1)} %bitcast.85), calls=%async_computation.6 | async-start | bytes 8388608
  51.0 5.0 %slice-start.1 = ((s8[6291456]{0:T(1024)(128)(4,1)}), s8[2097152]{0:T(1024)(128)(4,1)S(1)}, s32[]{:S(2)}) async-start(s8[6291456]{0:T(1024)(128)(4,1)} %bitcast.85), calls=%async_computation.7 | async-start | bytes 4194304
  51.0 7.1 %slice-start.2 = ((s8[6291456]{0:T(1024)(128)(4,1)}), s8[4194304]{0:T(1024)(128)(4,1)S(1)}, s32[]{:S(2)}) async-start(s8[6291456]{0:T(1024)(128)(4,1)} %bitcast.87), calls=%async_computation.8 | async-start | bytes 8388608
  56.0 2.1 %slice-start.3 = ((s8[6291456]{0:T(1024)(128)(4,1)}), s8[2097152]{0:T(1024)(128)(4,1)S(1)}, s32[]{:S(2)}) async-start(s8[6291456]{0:T(1024)(128)(4,1)} %bitcast.87), calls=%async_computation.9 | async-start | bytes 4194304
  58.2 8.3 %copy-start.1 = (bf16[4,4,12,384]{3,2,0,1:T(8,128)(2,1)S(1)}, bf16[4,4,12,384]{3,2,0,1:T(8,128)(2,1)}, u32[]{:S(2)}) copy-start(bf16[4,4,12,384]{3,2,0,1:T(8,128)(2,1)} %get-tuple-element.3) | copy-start | bytes 442372
  62.2 15.1 %all-to-all-start.3 = ((bf16[4,48,2048]{2,1,0:T(8,128)(2,1)}), bf16[4,48,2048]{2,1,0:T(8,128)(2,1)S(1)}, u32[]{:S(2)}, u32[]{:S(2)}) async-start(bf16[4,48,2048]{2,1,0:T(8,128)(2,1)} %copy.38), calls=%async_computation.3 | async-start | bytes 1572864 | tf_op jit(solution)/shard_map/all_to_all | solution.py:54
  65.7 64.5 %all-gather.3.cloned.1.call-start = ((), (), s32[]{:S(2)}) async-start(), calls=%async_computation.5 | async-start | bytes 1769472 | tf_op jit(solution)/shard_map/all_gather | solution.py:59
  77.4 15.1 %all-to-all-start.1 = ((bf16[4,48,2048]{2,1,0:T(8,128)(2,1)}), bf16[4,48,2048]{2,1,0:T(8,128)(2,1)S(1)}, u32[]{:S(2)}, u32[]{:S(2)}) async-start(bf16[4,48,2048]{2,1,0:T(8,128)(2,1)} %copy.34), calls=%async_computation.1 | async-start | bytes 1572864 | tf_op jit(solution)/shard_map/all_to_all | solution.py:42
  92.5 37.3 %all-to-all-start.4 = ((bf16[8,192,256]{2,1,0:T(8,128)(2,1)}), bf16[8,192,256]{2,1,0:T(8,128)(2,1)S(1)}, u32[]{:S(2)}, u32[]{:S(2)}) async-start(bf16[8,192,256]{2,1,0:T(8,128)(2,1)} %bitcast.82), calls=%async_computation.4 | async-start | bytes 1572864 | tf_op jit(solution)/shard_map/all_to_all | solution.py:60
Sparse Core Ops, SparseCore 0:
  68.8 59.6 all-gather.2

commit v2 on v1

--- a/solution.py
+++ b/solution.py
@@ -1,12 +1,17 @@
+import functools
+
 import jax
 import jax.numpy as jnp
+import numpy as np
 from jax import lax
+from jax.experimental import pallas as pl
+from jax.experimental.pallas import tpu as pltpu
 from jax.sharding import PartitionSpec as P
 
 CAP = 12
 
 
-def body(tokens, out_grad, expert_ids, combine_ints, w_gate, w_up, w_down):
+def plain_body(tokens, out_grad, expert_ids, combine_ints, w_gate, w_up, w_down):
     tok_rows, model_width = tokens.shape
     route_count = expert_ids.shape[1]
     groups = lax.axis_size("expert")
@@ -74,6 +79,266 @@
         axis=1,
     ).astype(jnp.bfloat16)
     return (combined, dinput, grad_share)
+
+
+MESH = pl.DeviceIdType.MESH
+TN = (((0,), (0,)), ((), ()))
+NN = (((1,), (0,)), ((), ()))
+NT = (((1,), (1,)), ((), ()))
+
+
+def mm(a, b, dims):
+    return lax.dot_general(a, b, dims, preferred_element_type=jnp.float32)
+
+
+def kernel(
+    groups,
+    parts,
+    tok_ref,
+    og_ref,
+    ids_ref,
+    ints_ref,
+    perm_ref,
+    wg_hbm,
+    wu_hbm,
+    wd_hbm,
+    comb_ref,
+    din_ref,
+    gd_ref,
+    wg,
+    wu,
+    wd,
+    x_out,
+    g_out,
+    x_in,
+    g_in,
+    rows,
+    grads,
+    o_out,
+    d_out,
+    o_in,
+    d_in,
+    stage,
+    gate_s,
+    up_s,
+    hid,
+    cot,
+    w_sem,
+    exp_send,
+    exp_recv,
+    dp_send,
+    dp_recv,
+):
+    bf16, f32 = jnp.bfloat16, jnp.float32
+    count, width = tok_ref.shape
+    local = wg_hbm.shape[0]
+    experts = groups * local
+    block = local * CAP
+    slots = groups * block
+    per = groups * CAP
+    cols = width // parts
+    me_e, me_d = lax.axis_index("expert"), lax.axis_index("dp")
+
+    def w_copy(which, hbm, vmem, l):
+        return pltpu.make_async_copy(hbm.at[l], vmem.at[l], w_sem.at[which, l])
+
+    for l in range(local):
+        w_copy(0, wg_hbm, wg, l).start()
+        w_copy(1, wu_hbm, wu, l).start()
+    for l in range(local):
+        w_copy(2, wd_hbm, wd, l).start()
+
+    def expert_at(k):
+        return {"expert": lax.rem(me_e + k + groups, groups)}
+
+    def dp_at(k):
+        return {"dp": lax.rem(me_d + k, parts)}
+
+    barrier = pltpu.get_barrier_semaphore()
+    for k in range(1, groups):
+        pl.semaphore_signal(barrier, inc=1, device_id=expert_at(k), device_id_type=MESH)
+    for k in range(1, parts):
+        pl.semaphore_signal(barrier, inc=1, device_id=dp_at(k), device_id_type=MESH)
+
+    ids = ids_ref[...]
+    hot = (ids == lax.broadcasted_iota(jnp.int32, (count, experts), 1)).astype(f32)
+    earlier = (
+        lax.broadcasted_iota(jnp.int32, (count, count), 1)
+        < lax.broadcasted_iota(jnp.int32, (count, count), 0)
+    ).astype(f32)
+    before = mm(earlier.astype(bf16), hot.astype(bf16), NN)
+    rank = jnp.sum(before * hot, axis=1, keepdims=True).astype(jnp.int32)
+    shifted = ids - me_e * local
+    shifted = jnp.where(shifted < 0, shifted + experts, shifted)
+    slot = shifted * CAP + rank
+    pick = (slot == lax.broadcasted_iota(jnp.int32, (count, slots), 1)).astype(f32).astype(bf16)
+    ints = ints_ref[...].astype(f32)
+    weight = ints[:, :1] / jnp.sum(ints, axis=1, keepdims=True)
+
+    def to_expert(row, src, dst, k, toward):
+        piece = pl.ds(k * block, block)
+        return pltpu.make_async_remote_copy(
+            src_ref=src.at[piece],
+            dst_ref=dst.at[piece],
+            send_sem=exp_send.at[row, k],
+            recv_sem=exp_recv.at[row, k],
+            device_id=expert_at(k if toward else -k),
+            device_id_type=MESH,
+        )
+
+    ring = sorted(range(1, groups), key=lambda k: abs(2 * k - groups))
+
+    def post(row, src, dst, value, toward):
+        src[...] = value.astype(bf16)
+        dst[pl.ds(0, block)] = src[pl.ds(0, block)]
+        for k in ring:
+            to_expert(row, src, dst, k, toward).start()
+
+    def arrived(row, src, dst, toward):
+        for k in ring:
+            to_expert(row, src, dst, k, toward).wait_recv()
+
+    def to_dp(row, src, dst, k):
+        return pltpu.make_async_remote_copy(
+            src_ref=src,
+            dst_ref=dst.at[k],
+            send_sem=dp_send.at[row, k],
+            recv_sem=dp_recv.at[row, k],
+            device_id=dp_at(k),
+            device_id_type=MESH,
+        )
+
+    x_value = mm(pick, tok_ref[...], TN)
+    pl.semaphore_wait(barrier, groups + parts - 2)
+    post(0, x_out, x_in, x_value, True)
+    scaled = (weight * og_ref[...].astype(f32)).astype(bf16)
+    post(1, g_out, g_in, mm(pick, scaled, TN), True)
+
+    arrived(0, x_out, x_in, True)
+    rows[...] = mm(perm_ref[...], x_in[...], NN).astype(bf16)
+
+    def forward(l, carry):
+        w_copy(0, wg_hbm, wg, l).wait()
+        w_copy(1, wu_hbm, wu, l).wait()
+        piece = pl.ds(pl.multiple_of(l * per, per), per)
+        x = rows[piece]
+        gate = mm(x, wg[l], NN)
+        up = mm(x, wu[l], NN)
+        gate_s[piece] = gate
+        up_s[piece] = up
+        hid[0, piece] = (gate * jax.nn.sigmoid(gate) * up).astype(bf16)
+        return carry
+
+    lax.fori_loop(0, local, forward, 0)
+    for k in range(1, parts):
+        to_dp(0, hid.at[0], hid, k).start()
+
+    arrived(1, g_out, g_in, True)
+    grads[...] = mm(perm_ref[...], g_in[...], NN).astype(bf16)
+
+    def columns(k):
+        return pl.ds(pl.multiple_of(lax.rem(me_d + k, parts) * cols, cols), cols)
+
+    for k in range(1, parts):
+        to_dp(1, grads.at[:, columns(k)], cot, k).start()
+    cot[0] = grads[:, columns(0)]
+
+    def down(l, carry):
+        w_copy(2, wd_hbm, wd, l).wait()
+        piece = pl.ds(pl.multiple_of(l * per, per), per)
+        stage[piece] = mm(hid[0, piece], wd[l], NN).astype(bf16)
+        return carry
+
+    lax.fori_loop(0, local, down, 0)
+    post(2, o_out, o_in, mm(perm_ref[...], stage[...], TN), False)
+
+    def backward(l, carry):
+        piece = pl.ds(pl.multiple_of(l * per, per), per)
+        dh = mm(grads[piece], wd[l], NT)
+        gate, up = gate_s[piece], up_s[piece]
+        sig = jax.nn.sigmoid(gate)
+        d_gate = (dh * up * sig * (1.0 + gate * (1.0 - sig))).astype(bf16)
+        d_up = (dh * (gate * sig)).astype(bf16)
+        stage[piece] = (mm(d_gate, wg[l], NT) + mm(d_up, wu[l], NT)).astype(bf16)
+        return carry
+
+    lax.fori_loop(0, local, backward, 0)
+    post(3, d_out, d_in, mm(perm_ref[...], stage[...], TN), False)
+
+    arrived(2, o_out, o_in, False)
+    comb_ref[...] = (weight * mm(pick, o_in[...], NN)).astype(bf16)
+
+    for k in range(1, parts):
+        to_dp(0, hid.at[0], hid, k).wait_recv()
+    for k in range(1, parts):
+        to_dp(1, grads.at[:, columns(k)], cot, k).wait_recv()
+
+    def down_grad(l, carry):
+        piece = pl.ds(pl.multiple_of(l * per, per), per)
+        h = hid[:, piece].reshape(parts * per, hid.shape[2])
+        c = cot[:, piece].reshape(parts * per, cols)
+        gd_ref[l] = mm(h, c, TN)
+        return carry
+
+    lax.fori_loop(0, local, down_grad, 0)
+
+    arrived(3, d_out, d_in, False)
+    din_ref[...] = mm(pick, d_in[...], NN).astype(bf16)
+
+    for k in ring:
+        to_expert(0, x_out, x_in, k, True).wait_send()
+        to_expert(1, g_out, g_in, k, True).wait_send()
+        to_expert(2, o_out, o_in, k, False).wait_send()
+        to_expert(3, d_out, d_in, k, False).wait_send()
+    for k in range(1, parts):
+        to_dp(0, hid.at[0], hid, k).wait_send()
+        to_dp(1, grads.at[:, columns(k)], cot, k).wait_send()
+
+
+def body(tokens, out_grad, expert_ids, combine_ints, w_gate, w_up, w_down):
+    count, width = tokens.shape
+    groups, parts = lax.axis_size("expert"), lax.axis_size("dp")
+    local, _, inner = w_gate.shape
+    block, per, cols = local * CAP, groups * CAP, width // parts
+    if expert_ids.shape[1] != 1 or block % 16 or per % 16 or cols % 128:
+        return plain_body(tokens, out_grad, expert_ids, combine_ints, w_gate, w_up, w_down)
+    slots = groups * block
+    order = np.arange(slots).reshape(groups, local, CAP).transpose(1, 0, 2).reshape(-1)
+    perm = jnp.asarray(np.eye(slots, dtype=np.float32)[order], jnp.bfloat16)
+    bf16, f32 = jnp.bfloat16, jnp.float32
+    vmem = pl.BlockSpec(memory_space=pltpu.VMEM)
+    hbm = pl.BlockSpec(memory_space=pl.ANY)
+    wide = pltpu.VMEM((slots, width), bf16)
+    return pl.pallas_call(
+        functools.partial(kernel, groups, parts),
+        out_shape=(
+            jax.ShapeDtypeStruct((count, width), bf16),
+            jax.ShapeDtypeStruct((count, width), bf16),
+            jax.ShapeDtypeStruct((local, inner, cols), f32),
+        ),
+        in_specs=[vmem] * 5 + [hbm] * 3,
+        out_specs=(vmem, vmem, vmem),
+        scratch_shapes=[
+            pltpu.VMEM(w_gate.shape, bf16),
+            pltpu.VMEM(w_up.shape, bf16),
+            pltpu.VMEM(w_down.shape, bf16),
+        ]
+        + [wide] * 11
+        + [
+            pltpu.VMEM((slots, inner), f32),
+            pltpu.VMEM((slots, inner), f32),
+            pltpu.VMEM((parts, slots, inner), bf16),
+            pltpu.VMEM((parts, slots, cols), bf16),
+            pltpu.SemaphoreType.DMA((3, local)),
+            pltpu.SemaphoreType.DMA((4, groups)),
+            pltpu.SemaphoreType.DMA((4, groups)),
+            pltpu.SemaphoreType.DMA((2, parts)),
+            pltpu.SemaphoreType.DMA((2, parts)),
+        ],
+        compiler_params=pltpu.CompilerParams(
+            collective_id=0, has_side_effects=True, vmem_limit_bytes=58 * 2**20
+        ),
+    )(tokens, out_grad, expert_ids, combine_ints, perm, w_gate, w_up, w_down)
 
 
 def solution(mesh):

time: 141 us -> 75.2 us (0.53)
  the two profiles are of different devices: /device:TPU:0 before, /device:TPU:11 now
where the time goes in v2:
time: 75.2 us; the launch traced here: 74.9 us
  Pallas kernels  65 us (86%)
  local copies, waits for them, and re-layouts  9.22 us (12%)
    pallas_call x1, Pallas kernels, body(): pl.pallas_call(functools.partial(kernel, groups, parts), out_shape=(jax.S...  65 us
    unnamed x5, local copies, waits for them, and re-layouts  9.22 us

profile of v2, /device:TPU:11, one launch (start us, length us, event | category | flops | bytes accessed | tf_op | source)
XLA Modules:
  0.0 74.9 jit_solution(8058015057650714007)
XLA Ops:
  0.6 1.4 %copy.11.ids_ref = s32[128,1]{1,0:T(8,128)} copy(s32[128,1]{0,1:T(1,128)} %param.10) | data formatting | bytes 1024 | tf_op args[2]
  2.0 1.4 %copy.12.ints_ref = s32[128,8]{1,0:T(8,128)} copy(s32[128,8]{0,1:T(8,128)} %param.11) | data formatting | bytes 8192 | tf_op args[3]
  3.4 65.0 %shard_map.103 = (bf16[128,2048]{1,0:T(8,128)(2,1)}, bf16[128,2048]{1,0:T(8,128)(2,1)}, f32[4,384,256]{2,1,0:T(8,128)}) custom-call(bf16[128,2048]{1,0:T(8,128)(2,1)} %tok_ref.1, bf16[128,2048]{1,0:T(8,128)(2,1)} %og_ref.1, s32[128,1]{1,0:T(8,128)} %copy.11.ids_ref, s32[128,8]{1,0:T(8,128)} %copy.12.ints_ref, bf16[192,192]{1,0:T(8,128)(2,1)} %constant.2.clone.perm_ref, ...), custom_call_target="tpu_custom_call" | custom-call | tf_op jit(solution)/shard_map/pallas_call | solution.py:312
  68.5 1.9 %copy.16 = bf16[128,2048]{1,0:T(8,128)(2,1)} copy(bf16[128,2048]{1,0:T(8,128)(2,1)} %get-tuple-element.6) | data formatting | bytes 1048576
  70.4 1.9 %copy.17 = bf16[128,2048]{1,0:T(8,128)(2,1)} copy(bf16[128,2048]{1,0:T(8,128)(2,1)} %get-tuple-element.7) | data formatting | bytes 1048576
  72.2 2.7 %copy.18 = f32[4,384,256]{2,1,0:T(8,128)} copy(f32[4,384,256]{2,1,0:T(8,128)} %get-tuple-element.8) | data formatting | bytes 3145728

commit v3 on v2

--- a/solution.py
+++ b/solution.py
@@ -96,8 +96,8 @@
     parts,
     tok_ref,
     og_ref,
-    ids_ref,
-    ints_ref,
+    routing_ref,
+    base_ref,
     perm_ref,
     wg_hbm,
     wu_hbm,
@@ -123,11 +123,14 @@
     up_s,
     hid,
     cot,
+    cot_rows,
     w_sem,
     exp_send,
     exp_recv,
-    dp_send,
-    dp_recv,
+    hid_send,
+    hid_recv,
+    cot_send,
+    cot_recv,
 ):
     bf16, f32 = jnp.bfloat16, jnp.float32
     count, width = tok_ref.shape
@@ -148,31 +151,37 @@
     for l in range(local):
         w_copy(2, wd_hbm, wd, l).start()
 
-    def expert_at(k):
-        return {"expert": lax.rem(me_e + k + groups, groups)}
-
-    def dp_at(k):
-        return {"dp": lax.rem(me_d + k, parts)}
+    def partner(i):
+        return i + 1 - 2 * lax.rem(i, 2)
+
+    def ahead(i, slot, n):
+        there = lax.rem(i + slot - slot % 2, n)
+        return partner(there) if slot % 2 else there
+
+    def behind(i, slot, n):
+        return lax.rem((partner(i) if slot % 2 else i) - (slot - slot % 2) + n, n)
 
     barrier = pltpu.get_barrier_semaphore()
     for k in range(1, groups):
-        pl.semaphore_signal(barrier, inc=1, device_id=expert_at(k), device_id_type=MESH)
+        pl.semaphore_signal(barrier, inc=1, device_id={"expert": ahead(me_e, k, groups)}, device_id_type=MESH)
     for k in range(1, parts):
-        pl.semaphore_signal(barrier, inc=1, device_id=dp_at(k), device_id_type=MESH)
-
-    ids = ids_ref[...]
-    hot = (ids == lax.broadcasted_iota(jnp.int32, (count, experts), 1)).astype(f32)
+        pl.semaphore_signal(barrier, inc=1, device_id={"dp": ahead(me_d, k, parts)}, device_id_type=MESH)
+
+    routing = routing_ref[...]
+    side = lax.rem(me_e, 2)
+    shifted = routing[:, :1] - (me_e - side) * local
+    shifted = jnp.where(shifted < 0, shifted + experts, shifted)
+    hot = (shifted == lax.broadcasted_iota(jnp.int32, (count, experts), 1)).astype(f32)
     earlier = (
         lax.broadcasted_iota(jnp.int32, (count, count), 1)
         < lax.broadcasted_iota(jnp.int32, (count, count), 0)
     ).astype(f32)
     before = mm(earlier.astype(bf16), hot.astype(bf16), NN)
-    rank = jnp.sum(before * hot, axis=1, keepdims=True).astype(jnp.int32)
-    shifted = ids - me_e * local
-    shifted = jnp.where(shifted < 0, shifted + experts, shifted)
-    slot = shifted * CAP + rank
+    odd = side.astype(f32)
+    base = base_ref[0:1] * (1.0 - odd) + base_ref[1:2] * odd
+    slot = jnp.sum((before + base) * hot, axis=1, keepdims=True).astype(jnp.int32)
     pick = (slot == lax.broadcasted_iota(jnp.int32, (count, slots), 1)).astype(f32).astype(bf16)
-    ints = ints_ref[...].astype(f32)
+    ints = routing[:, 1:].astype(f32)
     weight = ints[:, :1] / jnp.sum(ints, axis=1, keepdims=True)
 
     def to_expert(row, src, dst, k, toward):
@@ -182,11 +191,11 @@
             dst_ref=dst.at[piece],
             send_sem=exp_send.at[row, k],
             recv_sem=exp_recv.at[row, k],
-            device_id=expert_at(k if toward else -k),
+            device_id={"expert": (ahead if toward else behind)(me_e, k, groups)},
             device_id_type=MESH,
         )
 
-    ring = sorted(range(1, groups), key=lambda k: abs(2 * k - groups))
+    ring = [*range(2, groups), 1]
 
     def post(row, src, dst, value, toward):
         src[...] = value.astype(bf16)
@@ -198,21 +207,44 @@
         for k in ring:
             to_expert(row, src, dst, k, toward).wait_recv()
 
-    def to_dp(row, src, dst, k):
+    def hid_copy(l, slot):
+        piece = pl.ds(pl.multiple_of(l * per, per), per)
+        relay = slot % 2
         return pltpu.make_async_remote_copy(
-            src_ref=src,
-            dst_ref=dst.at[k],
-            send_sem=dp_send.at[row, k],
-            recv_sem=dp_recv.at[row, k],
-            device_id=dp_at(k),
+            src_ref=hid.at[slot - relay if relay else 0, piece],
+            dst_ref=hid.at[slot, piece],
+            send_sem=hid_send.at[l, slot],
+            recv_sem=hid_recv.at[l, slot],
+            device_id={"dp": partner(me_d) if relay else ahead(me_d, slot, parts)},
             device_id_type=MESH,
         )
+
+    def columns(slot):
+        return pl.ds(pl.multiple_of(ahead(me_d, slot, parts) * cols, cols), cols)
+
+    def cot_copy(j, slot):
+        piece = pl.ds(j * block, block)
+        return pltpu.make_async_remote_copy(
+            src_ref=g_in.at[piece, columns(slot)],
+            dst_ref=cot.at[slot, piece],
+            send_sem=cot_send.at[j, slot],
+            recv_sem=cot_recv.at[j, slot],
+            device_id={"dp": ahead(me_d, slot, parts)},
+            device_id_type=MESH,
+        )
+
+    def send_columns(j):
+        for slot in range(1, parts):
+            cot_copy(j, slot).start()
 
     x_value = mm(pick, tok_ref[...], TN)
     pl.semaphore_wait(barrier, groups + parts - 2)
     post(0, x_out, x_in, x_value, True)
     scaled = (weight * og_ref[...].astype(f32)).astype(bf16)
     post(1, g_out, g_in, mm(pick, scaled, TN), True)
+    send_columns(0)
+    to_expert(1, g_out, g_in, 1, True).wait_recv()
+    send_columns(1)
 
     arrived(0, x_out, x_in, True)
     rows[...] = mm(perm_ref[...], x_in[...], NN).astype(bf16)
@@ -227,22 +259,11 @@
         gate_s[piece] = gate
         up_s[piece] = up
         hid[0, piece] = (gate * jax.nn.sigmoid(gate) * up).astype(bf16)
+        for slot in (*range(2, parts, 2), 1):
+            hid_copy(l, slot).start()
         return carry
 
     lax.fori_loop(0, local, forward, 0)
-    for k in range(1, parts):
-        to_dp(0, hid.at[0], hid, k).start()
-
-    arrived(1, g_out, g_in, True)
-    grads[...] = mm(perm_ref[...], g_in[...], NN).astype(bf16)
-
-    def columns(k):
-        return pl.ds(pl.multiple_of(lax.rem(me_d + k, parts) * cols, cols), cols)
-
-    for k in range(1, parts):
-        to_dp(1, grads.at[:, columns(k)], cot, k).start()
-    cot[0] = grads[:, columns(0)]
-
     def down(l, carry):
         w_copy(2, wd_hbm, wd, l).wait()
         piece = pl.ds(pl.multiple_of(l * per, per), per)
@@ -251,6 +272,12 @@
 
     lax.fori_loop(0, local, down, 0)
     post(2, o_out, o_in, mm(perm_ref[...], stage[...], TN), False)
+
+    for j in range(2, groups):
+        to_expert(1, g_out, g_in, j, True).wait_recv()
+        send_columns(j)
+    grads[...] = mm(perm_ref[...], g_in[...], NN).astype(bf16)
+    cot[0] = g_in[:, columns(0)]
 
     def backward(l, carry):
         piece = pl.ds(pl.multiple_of(l * per, per), per)
@@ -265,18 +292,33 @@
     lax.fori_loop(0, local, backward, 0)
     post(3, d_out, d_in, mm(perm_ref[...], stage[...], TN), False)
 
+    def relay(l, carry):
+        for slot in range(2, parts, 2):
+            hid_copy(l, slot).wait_recv()
+            hid_copy(l, slot + 1).start()
+        return carry
+
+    lax.fori_loop(0, local, relay, 0)
+
     arrived(2, o_out, o_in, False)
     comb_ref[...] = (weight * mm(pick, o_in[...], NN)).astype(bf16)
 
-    for k in range(1, parts):
-        to_dp(0, hid.at[0], hid, k).wait_recv()
-    for k in range(1, parts):
-        to_dp(1, grads.at[:, columns(k)], cot, k).wait_recv()
+    for j in range(groups):
+        for slot in range(1, parts):
+            cot_copy(j, slot).wait_recv()
+
+    def regroup(p, carry):
+        cot_rows[p] = mm(perm_ref[...], cot[p], NN).astype(bf16)
+        return carry
+
+    lax.fori_loop(0, parts, regroup, 0)
 
     def down_grad(l, carry):
+        for slot in range(1, parts, 2):
+            hid_copy(l, slot).wait_recv()
         piece = pl.ds(pl.multiple_of(l * per, per), per)
         h = hid[:, piece].reshape(parts * per, hid.shape[2])
-        c = cot[:, piece].reshape(parts * per, cols)
+        c = cot_rows[:, piece].reshape(parts * per, cols)
         gd_ref[l] = mm(h, c, TN)
         return carry
 
@@ -290,9 +332,16 @@
         to_expert(1, g_out, g_in, k, True).wait_send()
         to_expert(2, o_out, o_in, k, False).wait_send()
         to_expert(3, d_out, d_in, k, False).wait_send()
-    for k in range(1, parts):
-        to_dp(0, hid.at[0], hid, k).wait_send()
-        to_dp(1, grads.at[:, columns(k)], cot, k).wait_send()
+
+    def sent(l, carry):
+        for slot in range(1, parts):
+            hid_copy(l, slot).wait_send()
+        return carry
+
+    lax.fori_loop(0, local, sent, 0)
+    for j in range(groups):
+        for slot in range(1, parts):
+            cot_copy(j, slot).wait_send()
 
 
 def body(tokens, out_grad, expert_ids, combine_ints, w_gate, w_up, w_down):
@@ -300,11 +349,15 @@
     groups, parts = lax.axis_size("expert"), lax.axis_size("dp")
     local, _, inner = w_gate.shape
     block, per, cols = local * CAP, groups * CAP, width // parts
-    if expert_ids.shape[1] != 1 or block % 16 or per % 16 or cols % 128:
+    if expert_ids.shape[1] != 1 or groups % 2 or parts % 2 or block % 16 or per % 16 or cols % 128:
         return plain_body(tokens, out_grad, expert_ids, combine_ints, w_gate, w_up, w_down)
     slots = groups * block
     order = np.arange(slots).reshape(groups, local, CAP).transpose(1, 0, 2).reshape(-1)
     perm = jnp.asarray(np.eye(slots, dtype=np.float32)[order], jnp.bfloat16)
+    unit = np.arange(groups * local)
+    swapped = (unit // local ^ 1) * local + unit % local
+    base = jnp.asarray(np.stack([unit, swapped]) * CAP, jnp.float32)
+    routing = jnp.concatenate([expert_ids, combine_ints], axis=1)
     bf16, f32 = jnp.bfloat16, jnp.float32
     vmem = pl.BlockSpec(memory_space=pltpu.VMEM)
     hbm = pl.BlockSpec(memory_space=pl.ANY)
@@ -329,16 +382,19 @@
             pltpu.VMEM((slots, inner), f32),
             pltpu.VMEM((parts, slots, inner), bf16),
             pltpu.VMEM((parts, slots, cols), bf16),
+            pltpu.VMEM((parts, slots, cols), bf16),
             pltpu.SemaphoreType.DMA((3, local)),
             pltpu.SemaphoreType.DMA((4, groups)),
             pltpu.SemaphoreType.DMA((4, groups)),
-            pltpu.SemaphoreType.DMA((2, parts)),
-            pltpu.SemaphoreType.DMA((2, parts)),
+            pltpu.SemaphoreType.DMA((local, parts)),
+            pltpu.SemaphoreType.DMA((local, parts)),
+            pltpu.SemaphoreType.DMA((groups, parts)),
+            pltpu.SemaphoreType.DMA((groups, parts)),
         ],
         compiler_params=pltpu.CompilerParams(
             collective_id=0, has_side_effects=True, vmem_limit_bytes=58 * 2**20
         ),
-    )(tokens, out_grad, expert_ids, combine_ints, perm, w_gate, w_up, w_down)
+    )(tokens, out_grad, routing, base, perm, w_gate, w_up, w_down)
 
 
 def solution(mesh):

time: 75.2 us -> 57.2 us (0.76)
  the two profiles are of different devices: /device:TPU:11 before, /device:TPU:0 now
where the time goes in v3:
time: 57.2 us; the launch traced here: 56.1 us
  Pallas kernels  47.6 us (83%)
  local copies, waits for them, and re-layouts  7.15 us (12%)
  other arithmetic  0.69 us (1%)
  between operations  0.64 us (1%)
    pallas_call x1, Pallas kernels, body(): pl.pallas_call(functools.partial(kernel, groups, parts), out_shape=(jax.S...  47.6 us
    unnamed x3, local copies, waits for them, and re-layouts  6.41 us

profile of v3, /device:TPU:0, one launch (start us, length us, event | category | flops | bytes accessed | tf_op | source)
XLA Modules:
  0.0 56.1 jit_solution(6077415746999237631)
XLA Ops:
  0.6 0.7 %pad_add_fusion = s32[128,9]{0,1:T(8,128)S(1)} fusion(s32[128,8]{0,1:T(8,128)} %param.12, s32[128,1]{0,1:T(1,128)} %param.11), kind=kLoop, calls=%fused_computation | loop fusion | flops 1152 | bytes 9216 | tf_op jit(solution)/shard_map/concatenate | solution.py:360
  1.3 0.7 %copy.14.routing_ref = s32[128,9]{1,0:T(8,128)} copy(s32[128,9]{0,1:T(8,128)S(1)} %pad_add_fusion) | data formatting | bytes 9216 | tf_op jit(solution)/shard_map/concatenate | solution.py:360
  2.1 47.6 %shard_map.112 = (bf16[128,2048]{1,0:T(8,128)(2,1)}, bf16[128,2048]{1,0:T(8,128)(2,1)}, f32[4,384,256]{2,1,0:T(8,128)}) custom-call(bf16[128,2048]{1,0:T(8,128)(2,1)} %tok_ref.1, bf16[128,2048]{1,0:T(8,128)(2,1)} %og_ref.1, s32[128,9]{1,0:T(8,128)} %copy.14.routing_ref, f32[2,16]{1,0:T(2,128)} %constant.5.clone.base_ref, ...), custom_call_target="tpu_custom_call" | custom-call | tf_op jit(solution)/shard_map/pallas_call | solution.py:365
  49.7 1.9 %copy.18 = bf16[128,2048]{1,0:T(8,128)(2,1)} copy(bf16[128,2048]{1,0:T(8,128)(2,1)} %get-tuple-element.6) | data formatting | bytes 1048576
  51.6 1.9 %copy.19 = bf16[128,2048]{1,0:T(8,128)(2,1)} copy(bf16[128,2048]{1,0:T(8,128)(2,1)} %get-tuple-element.7) | data formatting | bytes 1048576
  53.5 2.7 %copy.20 = f32[4,384,256]{2,1,0:T(8,128)} copy(f32[4,384,256]{2,1,0:T(8,128)} %get-tuple-element.8) | data formatting | bytes 3145728

commit v4 on v3

--- a/solution.py
+++ b/solution.py
@@ -94,14 +94,19 @@
 def kernel(
     groups,
     parts,
-    tok_ref,
-    og_ref,
+    tok_hbm,
+    og_hbm,
     routing_ref,
     base_ref,
     perm_ref,
     wg_hbm,
     wu_hbm,
     wd_hbm,
+    comb_hbm,
+    din_hbm,
+    gd_hbm,
+    tok_ref,
+    og_ref,
     comb_ref,
     din_ref,
     gd_ref,
@@ -125,6 +130,7 @@
     cot,
     cot_rows,
     w_sem,
+    io_sem,
     exp_send,
     exp_recv,
     hid_send,
@@ -133,7 +139,7 @@
     cot_recv,
 ):
     bf16, f32 = jnp.bfloat16, jnp.float32
-    count, width = tok_ref.shape
+    count, width = tok_hbm.shape
     local = wg_hbm.shape[0]
     experts = groups * local
     block = local * CAP
@@ -145,27 +151,32 @@
     def w_copy(which, hbm, vmem, l):
         return pltpu.make_async_copy(hbm.at[l], vmem.at[l], w_sem.at[which, l])
 
+    tok_copy = pltpu.make_async_copy(tok_hbm, tok_ref, io_sem.at[0])
+    og_copy = pltpu.make_async_copy(og_hbm, og_ref, io_sem.at[1])
+    tok_copy.start()
+    og_copy.start()
+
+    def partner(i):
+        return i + 1 - 2 * lax.rem(i, 2)
+
+    def ahead(i, slot, n):
+        there = lax.rem(i + slot - slot % 2, n)
+        return partner(there) if slot % 2 else there
+
+    def behind(i, slot, n):
+        return lax.rem((partner(i) if slot % 2 else i) - (slot - slot % 2) + n, n)
+
+    barrier = pltpu.get_barrier_semaphore()
+    for k in range(1, groups):
+        pl.semaphore_signal(barrier, inc=1, device_id={"expert": ahead(me_e, k, groups)}, device_id_type=MESH)
+    for k in range(1, parts):
+        pl.semaphore_signal(barrier, inc=1, device_id={"dp": ahead(me_d, k, parts)}, device_id_type=MESH)
+
     for l in range(local):
         w_copy(0, wg_hbm, wg, l).start()
         w_copy(1, wu_hbm, wu, l).start()
     for l in range(local):
         w_copy(2, wd_hbm, wd, l).start()
-
-    def partner(i):
-        return i + 1 - 2 * lax.rem(i, 2)
-
-    def ahead(i, slot, n):
-        there = lax.rem(i + slot - slot % 2, n)
-        return partner(there) if slot % 2 else there
-
-    def behind(i, slot, n):
-        return lax.rem((partner(i) if slot % 2 else i) - (slot - slot % 2) + n, n)
-
-    barrier = pltpu.get_barrier_semaphore()
-    for k in range(1, groups):
-        pl.semaphore_signal(barrier, inc=1, device_id={"expert": ahead(me_e, k, groups)}, device_id_type=MESH)
-    for k in range(1, parts):
-        pl.semaphore_signal(barrier, inc=1, device_id={"dp": ahead(me_d, k, parts)}, device_id_type=MESH)
 
     routing = routing_ref[...]
     side = lax.rem(me_e, 2)
@@ -237,9 +248,11 @@
         for slot in range(1, parts):
             cot_copy(j, slot).start()
 
+    tok_copy.wait()
     x_value = mm(pick, tok_ref[...], TN)
     pl.semaphore_wait(barrier, groups + parts - 2)
     post(0, x_out, x_in, x_value, True)
+    og_copy.wait()
     scaled = (weight * og_ref[...].astype(f32)).astype(bf16)
     post(1, g_out, g_in, mm(pick, scaled, TN), True)
     send_columns(0)
@@ -302,6 +315,8 @@
 
     arrived(2, o_out, o_in, False)
     comb_ref[...] = (weight * mm(pick, o_in[...], NN)).astype(bf16)
+    comb_copy = pltpu.make_async_copy(comb_ref, comb_hbm, io_sem.at[2])
+    comb_copy.start()
 
     for j in range(groups):
         for slot in range(1, parts):
@@ -312,6 +327,9 @@
         return carry
 
     lax.fori_loop(0, parts, regroup, 0)
+
+    def gd_copy(l):
+        return pltpu.make_async_copy(gd_ref.at[l], gd_hbm.at[l], w_sem.at[0, l])
 
     def down_grad(l, carry):
         for slot in range(1, parts, 2):
@@ -320,12 +338,15 @@
         h = hid[:, piece].reshape(parts * per, hid.shape[2])
         c = cot_rows[:, piece].reshape(parts * per, cols)
         gd_ref[l] = mm(h, c, TN)
+        gd_copy(l).start()
         return carry
 
     lax.fori_loop(0, local, down_grad, 0)
 
     arrived(3, d_out, d_in, False)
     din_ref[...] = mm(pick, d_in[...], NN).astype(bf16)
+    din_copy = pltpu.make_async_copy(din_ref, din_hbm, io_sem.at[3])
+    din_copy.start()
 
     for k in ring:
         to_expert(0, x_out, x_in, k, True).wait_send()
@@ -342,6 +363,30 @@
     for j in range(groups):
         for slot in range(1, parts):
             cot_copy(j, slot).wait_send()
+    comb_copy.wait()
+    din_copy.wait()
+    for l in range(local):
+        gd_copy(l).wait()
+
+
+def settle(count, *refs):
+    sources, results, held = refs[:count], refs[count : 2 * count], refs[2 * count : 3 * count]
+    sem = refs[-1]
+
+    def copy(i, j, stage):
+        rows = sources[i].shape[0] // 4
+        piece = pl.ds(j * rows, rows)
+        chain = sources[i].at[piece], held[i].at[piece], results[i].at[piece]
+        return pltpu.make_async_copy(chain[stage], chain[stage + 1], sem.at[stage, i, j])
+
+    pieces = [(i, j) for i in range(count) for j in range(4)]
+    for i, j in pieces:
+        copy(i, j, 0).start()
+    for i, j in pieces:
+        copy(i, j, 0).wait()
+        copy(i, j, 1).start()
+    for i, j in pieces:
+        copy(i, j, 1).wait()
 
 
 def body(tokens, out_grad, expert_ids, combine_ints, w_gate, w_up, w_down):
@@ -349,7 +394,7 @@
     groups, parts = lax.axis_size("expert"), lax.axis_size("dp")
     local, _, inner = w_gate.shape
     block, per, cols = local * CAP, groups * CAP, width // parts
-    if expert_ids.shape[1] != 1 or groups % 2 or parts % 2 or block % 16 or per % 16 or cols % 128:
+    if expert_ids.shape[1] != 1 or groups % 2 or parts % 2 or block % 16 or per % 16 or count % 64 or local % 4 or cols % 128:
         return plain_body(tokens, out_grad, expert_ids, combine_ints, w_gate, w_up, w_down)
     slots = groups * block
     order = np.arange(slots).reshape(groups, local, CAP).transpose(1, 0, 2).reshape(-1)
@@ -362,16 +407,21 @@
     vmem = pl.BlockSpec(memory_space=pltpu.VMEM)
     hbm = pl.BlockSpec(memory_space=pl.ANY)
     wide = pltpu.VMEM((slots, width), bf16)
-    return pl.pallas_call(
+    found = pl.pallas_call(
         functools.partial(kernel, groups, parts),
         out_shape=(
             jax.ShapeDtypeStruct((count, width), bf16),
             jax.ShapeDtypeStruct((count, width), bf16),
             jax.ShapeDtypeStruct((local, inner, cols), f32),
         ),
-        in_specs=[vmem] * 5 + [hbm] * 3,
-        out_specs=(vmem, vmem, vmem),
+        in_specs=[hbm] * 2 + [vmem] * 3 + [hbm] * 3,
+        out_specs=(hbm, hbm, hbm),
         scratch_shapes=[
+            pltpu.VMEM((count, width), bf16),
+            pltpu.VMEM((count, width), bf16),
+            pltpu.VMEM((count, width), bf16),
+            pltpu.VMEM((count, width), bf16),
+            pltpu.VMEM((local, inner, cols), f32),
             pltpu.VMEM(w_gate.shape, bf16),
             pltpu.VMEM(w_up.shape, bf16),
             pltpu.VMEM(w_down.shape, bf16),
@@ -384,6 +434,7 @@
             pltpu.VMEM((parts, slots, cols), bf16),
             pltpu.VMEM((parts, slots, cols), bf16),
             pltpu.SemaphoreType.DMA((3, local)),
+            pltpu.SemaphoreType.DMA((4,)),
             pltpu.SemaphoreType.DMA((4, groups)),
             pltpu.SemaphoreType.DMA((4, groups)),
             pltpu.SemaphoreType.DMA((local, parts)),
@@ -395,6 +446,15 @@
             collective_id=0, has_side_effects=True, vmem_limit_bytes=58 * 2**20
         ),
     )(tokens, out_grad, routing, base, perm, w_gate, w_up, w_down)
+    return pl.pallas_call(
+        functools.partial(settle, len(found)),
+        out_shape=tuple(jax.ShapeDtypeStruct(a.shape, a.dtype) for a in found),
+        in_specs=[hbm] * len(found),
+        out_specs=(hbm,) * len(found),
+        scratch_shapes=[pltpu.VMEM(a.shape, a.dtype) for a in found]
+        + [pltpu.SemaphoreType.DMA((2, len(found), 4))],
+        compiler_params=pltpu.CompilerParams(vmem_limit_bytes=58 * 2**20),
+    )(*found)
 
 
 def solution(mesh):

time: 57.2 us -> 52.5 us (0.918)
  local copies, waits for them, and re-layouts: 7.15 us -> 0.74 us
  Pallas kernels: 47.6 us -> 49.5 us
    unnamed x3 -> x0, local copies, waits for them, and re-layouts: 6.41 us -> none
    pallas_call x0 -> x1, Pallas kernels: none -> 2.76 us  [body(): pl.pallas_call(functools.partial(settle, len(found)), out_shape=tuple((ja...]
    pallas_call x1, Pallas kernels: 47.6 us -> 46.8 us  [body(): pl.pallas_call(functools.partial(kernel, groups, parts), out_shape=(jax.S...]
where the time goes in v4:
time: 52.5 us; the launch traced here: 51.6 us
  Pallas kernels  49.5 us (94%)
  local copies, waits for them, and re-layouts  0.74 us (1%)
  other arithmetic  0.69 us (1%)
  between operations  0.64 us (1%)
    pallas_call x1, Pallas kernels, body(): pl.pallas_call(functools.partial(kernel, groups, parts), out_shape=(jax.S...  46.8 us
    pallas_call x1, Pallas kernels, body(): pl.pallas_call(functools.partial(settle, len(found)), out_shape=tuple((ja...  2.76 us

profile of v4, /device:TPU:0, one launch (start us, length us, event | category | flops | bytes accessed | tf_op | source)
XLA Modules:
  0.0 51.6 jit_solution(479670401551108173)
XLA Ops:
  0.6 0.7 %pad_add_fusion = s32[128,9]{0,1:T(8,128)S(1)} fusion(s32[128,8]{0,1:T(8,128)} %param.12, s32[128,1]{0,1:T(1,128)} %param.11), kind=kLoop, calls=%fused_computation | loop fusion | flops 1152 | bytes 9216 | tf_op jit(solution)/shard_map/concatenate | solution.py:405
  1.3 0.7 %copy.14.routing_ref = s32[128,9]{1,0:T(8,128)} copy(s32[128,9]{0,1:T(8,128)S(1)} %pad_add_fusion) | data formatting | bytes 9216 | tf_op jit(solution)/shard_map/concatenate | solution.py:405
  2.1 46.8 %shard_map.112 = (bf16[128,2048]{1,0:T(8,128)(2,1)}, bf16[128,2048]{1,0:T(8,128)(2,1)}, f32[4,384,256]{2,1,0:T(8,128)}) custom-call(bf16[128,2048]{1,0:T(8,128)(2,1)} %tok_hbm.1, bf16[128,2048]{1,0:T(8,128)(2,1)} %og_hbm.1, s32[128,9]{1,0:T(8,128)} %copy.14.routing_ref, f32[2,16]{1,0:T(2,128)} %constant.5.clone.base_ref, ...), custom_call_target="tpu_custom_call" | custom-call | tf_op jit(solution)/shard_map/pallas_call | solution.py:410
  48.9 2.8 %shard_map.113 = (bf16[128,2048]{1,0:T(8,128)(2,1)}, bf16[128,2048]{1,0:T(8,128)(2,1)}, f32[4,384,256]{2,1,0:T(8,128)}) custom-call(bf16[128,2048]{1,0:T(8,128)(2,1)} %get-tuple-element.6.refs_0_, bf16[128,2048]{1,0:T(8,128)(2,1)} %get-tuple-element.7.refs_1_, f32[4,384,256]{2,1,0:T(8,128)} %get-tuple-element.8.refs_2_), custom_call_target="tpu_custom_call" | custom-call | tf_op jit(solution)/shard_map/pallas_call | solution.py:449
